TPU v7x, 32 devices: a whole 2x2x4 slice. The times are simulated.
32 devices in a mesh: fibre: 8 (over z, core), group: 4 (over y, x).
Axes of the slice: x: 2, y: 2, z: 4, core: 2. Of those that a mesh axis runs over, the one named last changes fastest.
Arguments:
- species_field: float32 [512, 32768], P('fibre', 'group'), may hold values from -45 to 45, as said below
- start_block: float32 [512, 64], replicated, may hold values from -4 to 4
Outputs:
- mode_basis: float32 [512, 64], replicated
- core_tensor: float32 [64, 32768], P(None, ('group', 'fibre'))
Inputs may be any that keep to these rules, and one draw needn't show every extreme that they name: `species_field`: float32 field values.
All inputs are finite; a program needn't handle non-finite values.
Results may differ from a plain program's by a relative error of at most 0.0003.
Values sent between devices are 32-bit elements; how exact they have to be, the bound alone decides.
A program may use at most 64 MiB of HBM per device.

v0:
```python
import jax
import jax.numpy as jnp
from jax import lax
from jax.sharding import PartitionSpec as P

ITERS = 3


highest_precision = lax.Precision.HIGHEST


def orthonormal(matrix):
    inner_gram = jnp.dot(matrix.T, matrix, precision=highest_precision)
    lower_factor = jnp.linalg.cholesky(inner_gram)
    return lax.linalg.triangular_solve(
        lower_factor, matrix, left_side=False, lower=True, transpose_a=True
    )


def on_device(species_field, start_block):
    fibres = lax.all_to_all(species_field, "fibre", split_axis=1, concat_axis=0, tiled=True)
    total_columns = fibres.shape[1] * lax.axis_size("fibre") * lax.axis_size("group")
    mode_basis = orthonormal(start_block)
    local_gram = jnp.dot(fibres, fibres.T, precision=highest_precision) / total_columns
    gram_matrix = lax.psum(local_gram, ("fibre", "group"))
    for iteration in range(ITERS):
        mode_basis = orthonormal(jnp.dot(gram_matrix, mode_basis, precision=highest_precision))
    core_tensor = jnp.dot(mode_basis.T, fibres, precision=highest_precision)
    return (mode_basis, core_tensor)


def solution(mesh):
    placed = (P("fibre", "group"), P())
    return jax.shard_map(
        on_device,
        mesh=mesh,
        in_specs=placed,
        out_specs=(P(), P(None, ("group", "fibre"))),
        check_vma=False,
    )
```

profile of v0, /device:TPU:0, one launch (start us, length us, event | category | flops | bytes accessed | tf_op | source)
XLA Modules:
  0.0 251.7 jit_solution(7081952542297371804)
XLA Ops:
  7.2 3.2 %copy.24 = f32[8,8,8,1024]{3,2,0,1:T(8,128)} copy(f32[8,8,8,1024]{3,2,1,0:T(8,128)} %bitcast.76) | data formatting | bytes 4194304 | tf_op jit(solution)/shard_map/all_to_all | solution.py:21
  10.4 6.3 %all-to-all-start = ((f32[64,8,1024]{2,0,1:T(8,128)}), f32[64,8,1024]{2,0,1:T(8,128)S(1)}, u32[]{:S(2)}, u32[]{:S(2)}) async-start(f32[64,8,1024]{2,0,1:T(8,128)} %bitcast.75), calls=%async_computation | async-start | bytes 4194304 | tf_op jit(solution)/shard_map/all_to_all | solution.py:21
  17.1 5.8 %cholesky.74 = f32[64,64]{1,0:T(8,128)S(1)} custom-call(f32[64,64]{1,0:T(8,128)S(1)} %fusion.11), custom_call_target="Cholesky" | custom-call | tf_op jit(solution)/shard_map/jit(cholesky)/cholesky | solution.py:14
  23.0 42.8 %all-to-all-done = f32[64,8,1024]{2,0,1:T(8,128)S(1)} async-done(((f32[64,8,1024]{2,0,1:T(8,128)}), f32[64,8,1024]{2,0,1:T(8,128)S(1)}, u32[]{:S(2)}, u32[]{:S(2)}) %all-to-all-start) | async-done | bytes 2097184 | tf_op jit(solution)/shard_map/all_to_all | solution.py:21
  65.8 4.6 %convolution_multiply_fusion = f32[512,512]{1,0:T(8,128)} fusion(f32[512,1024]{1,0:T(8,128)S(1)} %bitcast.73), kind=kOutput, calls=%fused_computation.1 | convolution fusion | flops 3221487616 | bytes 3145728 | tf_op jit(solution)/shard_map/dot_general | solution.py:24
  70.4 0.6 compare_reduce_fusion.3
  71.0 0.7 fusion
  71.7 4.9 %custom-call.8 = f32[1,64,64]{1,2,0:T(8,128)S(1)} custom-call(f32[1,64,64]{2,1,0:T(8,128)S(1)} %fusion), custom_call_target="InvertDiagBlocksLowerTriangular" | custom-call | tf_op jit(solution)/shard_map/triangular_solve/custom-call.0 | solution.py:15
  76.6 0.3 convolution_bitcast_fusion.3
  76.9 122.5 %all-reduce.2.cloned.1.call-done = f32[512,512]{1,0:T(8,128)} async-done(((f32[512,512]{1,0:T(8,128)}), f32[512,512]{1,0:T(8,128)}) %all-reduce.2.cloned.1.call-update) | async-done | bytes 1048592 | tf_op jit(solution)/shard_map/psum | solution.py:25
  199.4 2.4 fusion.19
  201.9 0.3 fusion.20
  202.2 5.8 %cholesky.85 = f32[64,64]{1,0:T(8,128)S(1)} custom-call(f32[64,64]{1,0:T(8,128)S(1)} %fusion.9), custom_call_target="Cholesky" | custom-call | tf_op jit(solution)/shard_map/jit(cholesky)/cholesky | solution.py:14
  208.1 0.6 compare_reduce_fusion.2
  208.7 0.7 fusion.1
  209.4 4.9 %custom-call.9 = f32[1,64,64]{1,2,0:T(8,128)S(1)} custom-call(f32[1,64,64]{2,1,0:T(8,128)S(1)} %fusion.1), custom_call_target="InvertDiagBlocksLowerTriangular" | custom-call | tf_op jit(solution)/shard_map/triangular_solve/custom-call.0 | solution.py:15
  214.3 0.3 convolution_bitcast_fusion.2
  214.7 1.1 fusion.21
  215.8 0.3 fusion.22
  216.2 5.8 %cholesky.96 = f32[64,64]{1,0:T(8,128)S(1)} custom-call(f32[64,64]{1,0:T(8,128)S(1)} %fusion.7), custom_call_target="Cholesky" | custom-call | tf_op jit(solution)/shard_map/jit(cholesky)/cholesky | solution.py:14
  222.0 0.6 compare_reduce_fusion.1
  222.7 0.7 fusion.2
  223.3 4.9 %custom-call.10 = f32[1,64,64]{1,2,0:T(8,128)S(1)} custom-call(f32[1,64,64]{2,1,0:T(8,128)S(1)} %fusion.2), custom_call_target="InvertDiagBlocksLowerTriangular" | custom-call | tf_op jit(solution)/shard_map/triangular_solve/custom-call.0 | solution.py:15
  228.2 0.3 convolution_bitcast_fusion.1
  228.6 1.3 fusion.23
  229.9 0.3 fusion.24
  230.3 5.8 %cholesky.107 = f32[64,64]{1,0:T(8,128)S(1)} custom-call(f32[64,64]{1,0:T(8,128)S(1)} %fusion.5), custom_call_target="Cholesky" | custom-call | tf_op jit(solution)/shard_map/jit(cholesky)/cholesky | solution.py:14
  236.2 0.6 compare_reduce_fusion
  236.8 0.7 fusion.3
  237.5 4.9 %custom-call.11 = f32[1,64,64]{1,2,0:T(8,128)S(1)} custom-call(f32[1,64,64]{2,1,0:T(8,128)S(1)} %fusion.3), custom_call_target="InvertDiagBlocksLowerTriangular" | custom-call | tf_op jit(solution)/shard_map/triangular_solve/custom-call.0 | solution.py:15
  242.4 0.3 convolution_bitcast_fusion
  242.7 2.1 fusion.25
  (21 shorter events, 0.8 us)
Async XLA Ops:
  7.2 9.6 %copy-start = (f32[512,64]{0,1:T(8,128)S(1)}, f32[512,64]{0,1:T(8,128)}, u32[]{:S(2)}) copy-start(f32[512,64]{0,1:T(8,128)} %param.6) | copy-start | bytes 393220
  10.4 55.4 %all-to-all-start = ((f32[64,8,1024]{2,0,1:T(8,128)}), f32[64,8,1024]{2,0,1:T(8,128)S(1)}, u32[]{:S(2)}, u32[]{:S(2)}) async-start(f32[64,8,1024]{2,0,1:T(8,128)} %bitcast.75), calls=%async_computation | async-start | bytes 4194304 | tf_op jit(solution)/shard_map/all_to_all | solution.py:21
  16.7 182.7 %all-reduce.2.cloned.1.call-start = ((), (), s32[]{:S(2)}) async-start(), calls=%async_computation.1 | async-start | bytes 2097152 | tf_op jit(solution)/shard_map/psum | solution.py:25
  199.4 15.2 %copy-start.1 = (f32[512,512]{1,0:T(8,128)S(1)}, f32[512,512]{1,0:T(8,128)}, u32[]{:S(2)}) copy-start(f32[512,512]{1,0:T(8,128)} %all-reduce.2.cloned.1.call-done) | copy-start | bytes 3145732
  242.7 2.1 copy-start.2
Sparse Core Ops, SparseCore 0:
  70.5 128.8 all-reduce.1
where the time goes:
time: 252 us
  waiting for transfers between devices  165 us (65%)
  other arithmetic  48.3 us (19%)
  between operations  14.2 us (6%)
  matrix products  13.9 us (6%)
  starting transfers between devices  6.36 us (3%)
  local copies, waits for them, and re-layouts  3.54 us (1%)
    psum x1, waiting for transfers between devices, on_device(): gram_matrix = lax.psum(local_gram, ('fibre', 'group'))  122 us
    all_to_all x1, waiting for transfers between devices, on_device(): lax.all_to_all(species_field, 'fibre', split_axis=1, concat_axis=0, tiled...  42.8 us
    another operation x12, other arithmetic, orthonormal(): lower_factor = jnp.linalg.cholesky(inner_gram)  26.1 us
    another operation x8, other arithmetic, orthonormal(): lax.linalg.triangular_solve(lower_factor, matrix, left_side=False, lower=...  22.2 us
    all_to_all x1, starting transfers between devices, on_device(): lax.all_to_all(species_field, 'fibre', split_axis=1, concat_axis=0, tiled...  6.33 us
  transfers between devices with their start and end apart: 2, of which 2 were waited for; matrix products, arithmetic and copies ran while one was open for 5% of the time, Pallas kernels for 0%

commit v1 on v0

v1 whole, which is shorter than its diff:
```python
import functools

import jax
import jax.numpy as jnp
from jax import lax
from jax.experimental import pallas as pl
from jax.experimental.pallas import tpu as pltpu
from jax.sharding import PartitionSpec as P

ITERS = 3
TILE = 128
MESH = pl.DeviceIdType.MESH
HIGHEST = lax.Precision.HIGHEST


def contract(a, b, dims):
    return lax.dot_general(
        a, b, (dims, ((), ())), precision=HIGHEST, preferred_element_type=jnp.float32
    )


def aligned(start, size):
    return pl.ds(pl.multiple_of(start, 8), size)


def gram_kernel(
    nf, ng, scale, field, fib, out, part, r1, r2, r3, own_sem,
    a_send, a_recv, c_send, c_recv, g_send, g_recv, z_send, z_recv,
):
    f = lax.axis_index("fibre")
    g = lax.axis_index("group")
    nz = nf // 2
    core = lax.rem(f, 2)
    z = f // 2
    mate = f + 1 - 2 * core
    rows, width = field.shape[0], fib.shape[1]
    order = fib.shape[0]
    half = part.shape[0] // 2
    quarter = half // ng
    piece = quarter // nz

    def fibre_peer(o):
        return lax.rem(f + o, nf)

    def group_peer(o):
        return lax.rem(g + o, ng)

    def z_peer(o):
        return lax.rem(z + o, nz)

    barrier = pltpu.get_barrier_semaphore()
    for o in range(1, nf):
        pl.semaphore_signal(barrier, inc=1, device_id=(fibre_peer(o), g), device_id_type=MESH)
    for o in range(1, ng):
        pl.semaphore_signal(barrier, inc=1, device_id=(f, group_peer(o)), device_id_type=MESH)
    pl.semaphore_wait(barrier, nf + ng - 2)

    here = fib.at[aligned(f * rows, rows), :]
    sends = []
    for o in sorted(range(1, nf), key=lambda o: abs(o - nf // 2)):
        peer = fibre_peer(o)
        copy = pltpu.make_async_remote_copy(
            src_ref=field.at[:, pl.ds(pl.multiple_of(peer * width, TILE), width)],
            dst_ref=here,
            send_sem=a_send.at[o],
            recv_sem=a_recv.at[o],
            device_id=(peer, g),
            device_id_type=MESH,
        )
        copy.start()
        sends.append(copy)
    own = pltpu.make_async_copy(
        field.at[:, pl.ds(pl.multiple_of(f * width, TILE), width)], here, own_sem
    )
    own.start()
    own.wait()
    for copy in sends:
        copy.wait()

    blocks = order // TILE
    base = 0
    for pair in range(0, blocks, 2):
        top = min(pair + 2, blocks)
        strip = contract(fib[pair * TILE:top * TILE, :], fib[:top * TILE, :], ((1,), (1,)))
        for i in range(pair, top):
            for j in range(i + 1):
                part[base:base + TILE, :] = strip[(i - pair) * TILE:(i - pair + 1) * TILE, j * TILE:(j + 1) * TILE]
                base += TILE
    if base < part.shape[0]:
        part[base:, :] = jnp.zeros((part.shape[0] - base, TILE), jnp.float32)

    copy = pltpu.make_async_remote_copy(
        src_ref=part.at[aligned((1 - core) * half, half), :], dst_ref=r1,
        send_sem=c_send.at[0], recv_sem=c_recv.at[0], device_id=(mate, g), device_id_type=MESH,
    )
    copy.start()
    copy.wait()
    mine = core * half
    part[aligned(mine, half), :] += r1[...]

    sends = []
    for o in range(1, ng):
        peer = group_peer(o)
        copy = pltpu.make_async_remote_copy(
            src_ref=part.at[aligned(mine + peer * quarter, quarter), :], dst_ref=r2.at[o],
            send_sem=g_send.at[o], recv_sem=g_recv.at[o], device_id=(f, peer), device_id_type=MESH,
        )
        copy.start()
        sends.append(copy)
    for copy in sends:
        copy.wait()
    mine = mine + g * quarter
    total = part[aligned(mine, quarter), :]
    for o in range(1, ng):
        total += r2[o]
    part[aligned(mine, quarter), :] = total

    sends = []
    for o in range(1, nz):
        peer = z_peer(o)
        copy = pltpu.make_async_remote_copy(
            src_ref=part.at[aligned(mine + peer * piece, piece), :], dst_ref=r3.at[o],
            send_sem=z_send.at[o], recv_sem=z_recv.at[o],
            device_id=(peer * 2 + core, g), device_id_type=MESH,
        )
        copy.start()
        sends.append(copy)
    for copy in sends:
        copy.wait()
    last = mine + z * piece
    total = part[aligned(last, piece), :]
    for o in range(1, nz):
        total += r3[o]
    out[aligned(last, piece), :] = total * scale

    block = out.at[aligned(last, piece), :]
    sends = []
    for o in range(1, nz):
        copy = pltpu.make_async_remote_copy(
            src_ref=block, dst_ref=block, send_sem=z_send.at[nz + o], recv_sem=z_recv.at[nz + o],
            device_id=(z_peer(o) * 2 + core, g), device_id_type=MESH,
        )
        copy.start()
        sends.append(copy)
    for copy in sends:
        copy.wait()
    block = out.at[aligned(mine, quarter), :]
    sends = []
    for o in range(1, ng):
        copy = pltpu.make_async_remote_copy(
            src_ref=block, dst_ref=block, send_sem=g_send.at[ng + o], recv_sem=g_recv.at[ng + o],
            device_id=(f, group_peer(o)), device_id_type=MESH,
        )
        copy.start()
        sends.append(copy)
    for copy in sends:
        copy.wait()
    block = out.at[aligned(core * half, half), :]
    copy = pltpu.make_async_remote_copy(
        src_ref=block, dst_ref=block, send_sem=c_send.at[1], recv_sem=c_recv.at[1],
        device_id=(mate, g), device_id_type=MESH,
    )
    copy.start()
    copy.wait()


def inverse_factor(a, rows_ref):
    n = a.shape[0]
    eye = (
        lax.broadcasted_iota(jnp.int32, (n, n), 0) == lax.broadcasted_iota(jnp.int32, (n, n), 1)
    ).astype(jnp.float32)
    w = jnp.concatenate([a, eye], axis=1)
    for k in range(0, n, 8):
        left = n - k
        cols = [jnp.broadcast_to(w[:, k + j:k + j + 1], (left, 2 * n)) for j in range(8)]
        for j in range(8):
            pivot = cols[j][j:j + 1, :]
            inv = lax.rsqrt(pivot)
            inv = inv * (1.5 - 0.5 * pivot * inv * inv)
            row = w[j:j + 1, :] * inv
            rows_ref[k + j:k + j + 1, :] = row
            below = cols[j] * inv
            w = w - below * row
            for m in range(j + 1, 8):
                cols[m] = cols[m] - below * (cols[m][j:j + 1, :] * inv)
        w = w[8:, :]
    return rows_ref[:, n:]


def basis_kernel(packed, fib, start, basis, core, gram, held, rows_ref):
    order = fib.shape[0]
    blocks = order // TILE
    base = 0
    for i in range(blocks):
        for j in range(i + 1):
            block = packed[base:base + TILE, :]
            gram[i * TILE:(i + 1) * TILE, j * TILE:(j + 1) * TILE] = block
            if j < i:
                gram[j * TILE:(j + 1) * TILE, i * TILE:(i + 1) * TILE] = block.T
            base += TILE
    held[...] = start[...]

    def orth(step, carry):
        matrix = held[...]
        inverse = inverse_factor(contract(matrix, matrix, ((0,), (0,))), rows_ref)
        q = contract(matrix, inverse, ((1,), (1,)))
        basis[...] = q

        @pl.when(step < ITERS)
        def _():
            held[...] = contract(gram[...], q, ((1,), (0,)))

        return carry

    lax.fori_loop(0, ITERS + 1, orth, 0)
    core[...] = contract(basis[...], fib[...], ((0,), (0,)))


def on_device(nf, ng, field, start):
    rows, columns = field.shape
    order, rank = start.shape
    width = columns // nf
    blocks = order // TILE
    step = 8 * nf * ng
    packed_rows = -(-(blocks * (blocks + 1) // 2 * TILE) // step) * step
    half = packed_rows // 2
    quarter = half // ng
    piece = quarter // (nf // 2)
    vmem = pl.BlockSpec(memory_space=pltpu.VMEM)
    f32 = jnp.float32
    dma = pltpu.SemaphoreType.DMA
    fib, packed = pl.pallas_call(
        functools.partial(gram_kernel, nf, ng, 1.0 / (columns * ng)),
        out_shape=(
            jax.ShapeDtypeStruct((order, width), f32),
            jax.ShapeDtypeStruct((packed_rows, TILE), f32),
        ),
        in_specs=[vmem],
        out_specs=(vmem, vmem),
        scratch_shapes=[
            pltpu.VMEM((packed_rows, TILE), f32),
            pltpu.VMEM((half, TILE), f32),
            pltpu.VMEM((ng, quarter, TILE), f32),
            pltpu.VMEM((nf // 2, piece, TILE), f32),
            dma,
            dma((nf,)), dma((nf,)),
            dma((2,)), dma((2,)),
            dma((2 * ng,)), dma((2 * ng,)),
            dma((nf,)), dma((nf,)),
        ],
        compiler_params=pltpu.CompilerParams(
            collective_id=0, has_side_effects=True, vmem_limit_bytes=48 * 2**20
        ),
        name="gram",
    )(field)
    return pl.pallas_call(
        basis_kernel,
        out_shape=(
            jax.ShapeDtypeStruct((order, rank), f32),
            jax.ShapeDtypeStruct((rank, width), f32),
        ),
        in_specs=[vmem] * 3,
        out_specs=(vmem, vmem),
        scratch_shapes=[
            pltpu.VMEM((order, order), f32),
            pltpu.VMEM((order, rank), f32),
            pltpu.VMEM((rank, 2 * rank), f32),
        ],
        compiler_params=pltpu.CompilerParams(vmem_limit_bytes=48 * 2**20),
        name="basis",
    )(packed, fib, start)


def solution(mesh):
    nf, ng = mesh.shape["fibre"], mesh.shape["group"]
    return jax.shard_map(
        functools.partial(on_device, nf, ng),
        mesh=mesh,
        in_specs=(P("fibre", "group"), P()),
        out_specs=(P(), P(None, ("group", "fibre"))),
        check_vma=False,
    )
```

time: 252 us -> 94.1 us (0.37)
  waiting for transfers between devices: 165 us -> 0 us
  Pallas kernels: 0 us -> 89.9 us
  other arithmetic: 48.3 us -> 0 us
  matrix products: 13.9 us -> 0 us
  between operations: 14.2 us -> 0.65 us
  starting transfers between devices: 6.36 us -> 0 us
    psum x1 -> x0, waiting for transfers between devices: 122 us -> none  [on_device(): gram_matrix = lax.psum(local_gram, ('fibre', 'group'))]
    pallas_call x0 -> x2, Pallas kernels: none -> 89.9 us  [the longest x1 74.9 us: on_device(): pl.pallas_call(functools.partial(gram_kernel, nf, ng, 1.0 / (columns * ng...]
    another operation x20 -> x0, other arithmetic: 48.3 us -> none  [the longest x12 26.1 us: orthonormal(): lower_factor = jnp.linalg.cholesky(inner_gram)]
    all_to_all x1 -> x0, waiting for transfers between devices: 42.8 us -> none  [on_device(): lax.all_to_all(species_field, 'fibre', split_axis=1, concat_axis=0, tiled...]
    dot_general x9 -> x0, matrix products: 12.6 us -> none  [the longest x3 4.9 us: on_device(): jnp.dot(gram_matrix, mode_basis, precision=highest_precision)]
    all_to_all x1 -> x0, starting transfers between devices: 6.33 us -> none  [on_device(): lax.all_to_all(species_field, 'fibre', split_axis=1, concat_axis=0, tiled...]
    all_to_all x1 -> x0, local copies, waits for them, and re-layouts: 3.23 us -> none  [on_device(): lax.all_to_all(species_field, 'fibre', split_axis=1, concat_axis=0, tiled...]
    unnamed x6 -> x3, local copies, waits for them, and re-layouts: 0.02 us -> 2.61 us
  transfers between devices with their start and end apart: 2 -> 0, of which waited for: 2 -> 0; matrix products, arithmetic and copies ran while one was open for 5% -> 0% of each run, Pallas kernels for 0% -> 0%
where the time goes in v1:
time: 94.1 us; the launch traced here: 93.9 us
  Pallas kernels  89.9 us (96%)
  local copies, waits for them, and re-layouts  3.39 us (4%)
    pallas_call x1, Pallas kernels, on_device(): pl.pallas_call(functools.partial(gram_kernel, nf, ng, 1.0 / (columns * ng...  74.9 us
    pallas_call x1, Pallas kernels, on_device(): pl.pallas_call(basis_kernel, out_shape=(jax.ShapeDtypeStruct((order, rank...  15 us
    unnamed x3, local copies, waits for them, and re-layouts  2.61 us

profile of v1, /device:TPU:0, one launch (start us, length us, event | category | flops | bytes accessed | tf_op | source)
XLA Modules:
  0.0 93.9 jit_solution(9287320006028396815)
XLA Ops:
  0.6 1.0 %copy.4.start = f32[512,64]{1,0:T(8,128)S(1)} copy(f32[512,64]{0,1:T(8,128)} %param.3) | data formatting | bytes 262144 | tf_op args[1]
  1.7 0.0 copy-start
  1.7 1.6 %copy-done = f32[64,8192]{1,0:T(8,128)S(1)} copy-done((f32[64,8192]{1,0:T(8,128)S(1)}, f32[64,8192]{1,0:T(8,128)}, u32[]{:S(2)}) %copy-start) | copy-done | bytes 2097176
  3.3 74.9 %gram.1 = (f32[512,1024]{1,0:T(8,128)S(1)}, f32[1280,128]{1,0:T(8,128)S(1)}) custom-call(f32[64,8192]{1,0:T(8,128)S(1)} %copy-done), custom_call_target="tpu_custom_call" | custom-call | tf_op jit(solution)/shard_map/gram/pallas_call | solution.py:232
  78.1 15.0 %basis.1 = (f32[512,64]{1,0:T(8,128)S(1)}, f32[64,1024]{1,0:T(8,128)}) custom-call(f32[1280,128]{1,0:T(8,128)S(1)} %get-tuple-element.4.packed, f32[512,1024]{1,0:T(8,128)S(1)} %get-tuple-element.5.fib, f32[512,64]{1,0:T(8,128)S(1)} %copy.4.start), custom_call_target="tpu_custom_call" | custom-call | tf_op jit(solution)/shard_map/basis/pallas_call | solution.py:256
  93.2 0.8 copy.5
Async XLA Ops:
  1.7 1.6 %copy-start = (f32[64,8192]{1,0:T(8,128)S(1)}, f32[64,8192]{1,0:T(8,128)}, u32[]{:S(2)}) copy-start(f32[64,8192]{1,0:T(8,128)} %field.1) | copy-start | bytes 6291460

commit v2 on v0

v2 whole, which is shorter than its diff:
```python
import functools

import jax
import jax.numpy as jnp
from jax import lax
from jax.experimental import pallas as pl
from jax.experimental.pallas import tpu as pltpu
from jax.sharding import PartitionSpec as P

ITERS = 3
TILE = 128
MESH = pl.DeviceIdType.MESH
HIGHEST = lax.Precision.HIGHEST


def contract(a, b, dims):
    return lax.dot_general(
        a, b, (dims, ((), ())), precision=HIGHEST, preferred_element_type=jnp.float32
    )


def aligned(start, size):
    return pl.ds(pl.multiple_of(start, 8), size)


def inverse_factor(a, rows_ref):
    n = a.shape[0]
    eye = (
        lax.broadcasted_iota(jnp.int32, (n, n), 0) == lax.broadcasted_iota(jnp.int32, (n, n), 1)
    ).astype(jnp.float32)
    w = jnp.concatenate([a, eye], axis=1)
    for k in range(0, n, 8):
        left = n - k
        cols = [jnp.broadcast_to(w[:, k + j:k + j + 1], (left, 2 * n)) for j in range(8)]
        for j in range(8):
            pivot = cols[j][j:j + 1, :]
            inv = lax.rsqrt(pivot)
            inv = inv * (1.5 - 0.5 * pivot * inv * inv)
            row = w[j:j + 1, :] * inv
            rows_ref[k + j:k + j + 1, :] = row
            below = cols[j] * inv
            w = w - below * row
            for m in range(j + 1, 8):
                cols[m] = cols[m] - below * (cols[m][j:j + 1, :] * inv)
        w = w[8:, :]
    return rows_ref[:, n:]


def kernel(
    nf, ng, chunks, parts, scale, field, start, basis, core_out,
    fib, part, out, r1, r2, r3, gram, held, rows_ref, own_sem,
    a_send, a_recv, c_send, c_recv, g_send, g_recv, z_send, z_recv,
):
    f = lax.axis_index("fibre")
    g = lax.axis_index("group")
    nz = nf // 2
    core = lax.rem(f, 2)
    z = f // 2
    mate = f + 1 - 2 * core
    rows, width = field.shape[0], fib.shape[1]
    order = fib.shape[0]
    span = width // chunks

    def remote(src, dst, send, recv, slot, device):
        copy = pltpu.make_async_remote_copy(
            src_ref=src, dst_ref=dst, send_sem=send.at[slot], recv_sem=recv.at[slot],
            device_id=device, device_id_type=MESH,
        )
        copy.start()
        return copy

    def fibre_peer(o):
        return lax.rem(f + o, nf)

    def group_device(o):
        return (f, lax.rem(g + o, ng))

    def z_device(o):
        return (lax.rem(z + o, nz) * 2 + core, g)

    barrier = pltpu.get_barrier_semaphore()
    for o in range(1, nf):
        pl.semaphore_signal(barrier, inc=1, device_id=(fibre_peer(o), g), device_id_type=MESH)
    for o in range(1, ng):
        pl.semaphore_signal(barrier, inc=1, device_id=group_device(o), device_id_type=MESH)
    pl.semaphore_wait(barrier, nf + ng - 2)

    far_first = sorted(range(1, nf), key=lambda o: abs(o - nf // 2))
    sends = []
    owns = []
    for c in range(chunks):
        here = fib.at[aligned(f * rows, rows), c * span:(c + 1) * span]
        sends.append([
            remote(
                field.at[:, pl.ds(pl.multiple_of(fibre_peer(o) * width + c * span, TILE), span)],
                here, a_send, a_recv, c * nf + o, (fibre_peer(o), g),
            )
            for o in far_first
        ])
        own = pltpu.make_async_copy(
            field.at[:, pl.ds(pl.multiple_of(f * width + c * span, TILE), span)], here, own_sem.at[c]
        )
        own.start()
        owns.append(own)

    def orth(matrix):
        inverse = inverse_factor(contract(matrix, matrix, ((1,), (1,))), rows_ref)
        return contract(inverse, matrix, ((1,), (0,)))

    held[...] = orth(start[...])

    def summed(p, first, size):
        half = size // 2
        quarter = half // ng
        piece = quarter // nz
        mine = first + core * half
        other = first + (1 - core) * half
        copy = remote(part.at[aligned(other, half), :], r1.at[0:half, :] if p == 0 else r1.at[r1.shape[0] - half:, :],
                      c_send, c_recv, 2 * p, (mate, g))
        yield
        copy.wait()
        base1 = 0 if p == 0 else r1.shape[0] - half
        part[aligned(mine, half), :] += r1[base1:base1 + half, :]

        at2 = 0 if p == 0 else r2.shape[1] - quarter
        copies = [
            remote(part.at[aligned(mine + lax.rem(g + o, ng) * quarter, quarter), :],
                   r2.at[o, at2:at2 + quarter, :], g_send, g_recv, 2 * p * ng + o, group_device(o))
            for o in range(1, ng)
        ]
        yield
        for copy in copies:
            copy.wait()
        mine = mine + g * quarter
        total = part[aligned(mine, quarter), :]
        for o in range(1, ng):
            total += r2[o, at2:at2 + quarter, :]
        part[aligned(mine, quarter), :] = total

        at3 = 0 if p == 0 else r3.shape[1] - piece
        copies = [
            remote(part.at[aligned(mine + lax.rem(z + o, nz) * piece, piece), :],
                   r3.at[o, at3:at3 + piece, :], z_send, z_recv, 2 * p * nz + o, z_device(o))
            for o in range(1, nz)
        ]
        yield
        for copy in copies:
            copy.wait()
        last = mine + z * piece
        total = part[aligned(last, piece), :]
        for o in range(1, nz):
            total += r3[o, at3:at3 + piece, :]
        out[aligned(last, piece), :] = total * scale

        block = out.at[aligned(last, piece), :]
        copies = [
            remote(block, block, z_send, z_recv, (2 * p + 1) * nz + o, z_device(o))
            for o in range(1, nz)
        ]
        yield
        for copy in copies:
            copy.wait()
        block = out.at[aligned(mine, quarter), :]
        copies = [
            remote(block, block, g_send, g_recv, (2 * p + 1) * ng + o, group_device(o))
            for o in range(1, ng)
        ]
        yield
        for copy in copies:
            copy.wait()
        block = out.at[aligned(first + core * half, half), :]
        copy = remote(block, block, c_send, c_recv, 2 * p + 1, (mate, g))
        yield
        copy.wait()

    blocks = order // TILE
    places = {}
    for pair in reversed(range(0, blocks, 2)):
        for i in range(pair, min(pair + 2, blocks)):
            for j in range(i + 1):
                places[i, j] = len(places) * TILE
    filled = len(places) * TILE
    if filled < part.shape[0]:
        part[filled:, :] = jnp.zeros((part.shape[0] - filled, TILE), jnp.float32)
    sums = []
    for c in range(chunks):
        for copy in sends[c]:
            copy.wait_recv()
        owns[c].wait()
        columns = slice(c * span, (c + 1) * span)
        done = 0
        for pair in reversed(range(0, blocks, 2)):
            top = min(pair + 2, blocks)
            strip = contract(fib[pair * TILE:top * TILE, columns], fib[:top * TILE, columns], ((1,), (1,)))
            for i in range(pair, top):
                for j in range(i + 1):
                    block = strip[(i - pair) * TILE:(i - pair + 1) * TILE, j * TILE:(j + 1) * TILE]
                    at = slice(places[i, j], places[i, j] + TILE)
                    part[at, :] = block if c == 0 else part[at, :] + block
                    done += TILE
            if c == chunks - 1:
                ready = part.shape[0] if done == filled else done
                while len(sums) < len(parts) and sum(parts[len(sums)]) <= ready:
                    step = summed(len(sums), *parts[len(sums)])
                    next(step)
                    sums.append(step)
    going = list(sums)
    while going:
        for step in list(going):
            try:
                next(step)
            except StopIteration:
                going.remove(step)

    for (i, j), at in places.items():
        block = out[at:at + TILE, :]
        gram[i * TILE:(i + 1) * TILE, j * TILE:(j + 1) * TILE] = block
        if j < i:
            gram[j * TILE:(j + 1) * TILE, i * TILE:(i + 1) * TILE] = block.T

    def iterate(step, carry):
        held[...] = orth(contract(held[...], gram[...], ((1,), (0,))))
        return carry

    lax.fori_loop(0, ITERS, iterate, 0)
    basis[...] = held[...]
    core_out[...] = contract(held[...], fib[...], ((1,), (0,)))
    for copies in sends:
        for copy in copies:
            copy.wait_send()


def on_device(nf, ng, field, start):
    rows, columns = field.shape
    order, rank = start.shape
    width = columns // nf
    chunks = 4
    blocks = order // TILE
    unit = 8 * nf * ng
    units = -(-(blocks * (blocks + 1) // 2 * TILE) // unit)
    sizes = [n * unit for n in (units - units // 2, units // 2) if n]
    parts = [(sum(sizes[:p]), size) for p, size in enumerate(sizes)]
    packed_rows = sum(sizes)
    vmem = pl.BlockSpec(memory_space=pltpu.VMEM)
    f32 = jnp.float32
    dma = pltpu.SemaphoreType.DMA
    basis, core = pl.pallas_call(
        functools.partial(kernel, nf, ng, chunks, parts, 1.0 / (columns * ng)),
        out_shape=(
            jax.ShapeDtypeStruct((rank, order), f32),
            jax.ShapeDtypeStruct((rank, width), f32),
        ),
        in_specs=[pl.BlockSpec(memory_space=pl.ANY), vmem],
        out_specs=(vmem, vmem),
        scratch_shapes=[
            pltpu.VMEM((order, width), f32),
            pltpu.VMEM((packed_rows, TILE), f32),
            pltpu.VMEM((packed_rows, TILE), f32),
            pltpu.VMEM((packed_rows // 2, TILE), f32),
            pltpu.VMEM((ng, packed_rows // 2 // ng, TILE), f32),
            pltpu.VMEM((nf // 2, packed_rows // nf // ng, TILE), f32),
            pltpu.VMEM((order, order), f32),
            pltpu.VMEM((rank, order), f32),
            pltpu.VMEM((rank, 2 * rank), f32),
            dma((chunks,)),
            dma((chunks * nf,)), dma((chunks * nf,)),
            dma((4,)), dma((4,)),
            dma((4 * ng,)), dma((4 * ng,)),
            dma((2 * nf,)), dma((2 * nf,)),
        ],
        compiler_params=pltpu.CompilerParams(
            collective_id=0, has_side_effects=True, vmem_limit_bytes=56 * 2**20
        ),
        name="subspace",
    )(field, start.T)
    return basis.T, core


def solution(mesh):
    nf, ng = mesh.shape["fibre"], mesh.shape["group"]
    return jax.shard_map(
        functools.partial(on_device, nf, ng),
        mesh=mesh,
        in_specs=(P("fibre", "group"), P()),
        out_specs=(P(), P(None, ("group", "fibre"))),
        check_vma=False,
    )
```

time: 252 us -> 88.5 us (0.35)
  waiting for transfers between devices: 165 us -> 0 us
  Pallas kernels: 0 us -> 84.5 us
  other arithmetic: 48.3 us -> 0 us
  matrix products: 13.9 us -> 0 us
  between operations: 14.2 us -> 0.64 us
  starting transfers between devices: 6.36 us -> 0 us
    psum x1 -> x0, waiting for transfers between devices: 122 us -> none  [on_device(): gram_matrix = lax.psum(local_gram, ('fibre', 'group'))]
    pallas_call x0 -> x1, Pallas kernels: none -> 84.5 us  [on_device(): pl.pallas_call(functools.partial(kernel, nf, ng, chunks, parts, 1.0 / (co...]
    another operation x20 -> x0, other arithmetic: 48.3 us -> none  [the longest x12 26.1 us: orthonormal(): lower_factor = jnp.linalg.cholesky(inner_gram)]
    all_to_all x1 -> x0, waiting for transfers between devices: 42.8 us -> none  [on_device(): lax.all_to_all(species_field, 'fibre', split_axis=1, concat_axis=0, tiled...]
    dot_general x9 -> x0, matrix products: 12.6 us -> none  [the longest x3 4.9 us: on_device(): jnp.dot(gram_matrix, mode_basis, precision=highest_precision)]
    all_to_all x1 -> x0, starting transfers between devices: 6.33 us -> none  [on_device(): lax.all_to_all(species_field, 'fibre', split_axis=1, concat_axis=0, tiled...]
    all_to_all x1 -> x0, local copies, waits for them, and re-layouts: 3.23 us -> none  [on_device(): lax.all_to_all(species_field, 'fibre', split_axis=1, concat_axis=0, tiled...]
    unnamed x6 -> x2, local copies, waits for them, and re-layouts: 0.02 us -> 3.24 us
  transfers between devices with their start and end apart: 2 -> 0, of which waited for: 2 -> 0; matrix products, arithmetic and copies ran while one was open for 5% -> 0% of each run, Pallas kernels for 0% -> 0%
where the time goes in v2:
time: 88.5 us; the launch traced here: 88.3 us
  Pallas kernels  84.5 us (95%)
  local copies, waits for them, and re-layouts  3.24 us (4%)
    pallas_call x1, Pallas kernels, on_device(): pl.pallas_call(functools.partial(kernel, nf, ng, chunks, parts, 1.0 / (co...  84.5 us
    unnamed x2, local copies, waits for them, and re-layouts  3.24 us

profile of v2, /device:TPU:0, one launch (start us, length us, event | category | flops | bytes accessed | tf_op | source)
XLA Modules:
  0.0 88.3 jit_solution(11353848608648912841)
XLA Ops:
  0.6 84.5 %subspace.1 = (f32[64,512]{1,0:T(8,128)}, f32[64,1024]{1,0:T(8,128)}) custom-call(f32[64,8192]{1,0:T(8,128)} %field.1, f32[64,512]{1,0:T(8,128)} %bitcast.2), custom_call_target="tpu_custom_call" | custom-call | tf_op jit(solution)/shard_map/subspace/pallas_call | solution.py:247
  85.1 1.6 %copy.6 = f32[512,64]{0,1:T(8,128)} copy(f32[512,64]{0,1:T(8,128)} %bitcast.3) | data formatting | bytes 262144
  86.7 1.7 %copy.7 = f32[64,1024]{1,0:T(8,128)} copy(f32[64,1024]{1,0:T(8,128)} %get-tuple-element.9) | data formatting | bytes 524288

commit v3 on v0

v3 whole, which is shorter than its diff:
```python
import functools

import jax
import jax.numpy as jnp
from jax import lax
from jax.experimental import pallas as pl
from jax.experimental.pallas import tpu as pltpu
from jax.sharding import PartitionSpec as P

ITERS = 3
TILE = 128
MESH = pl.DeviceIdType.MESH
HIGHEST = lax.Precision.HIGHEST


def contract(a, b, dims):
    return lax.dot_general(
        a, b, (dims, ((), ())), precision=HIGHEST, preferred_element_type=jnp.float32
    )


def aligned(start, size):
    return pl.ds(pl.multiple_of(start, 8), size)


def inverse_factor(a, rows_ref):
    n = a.shape[0]
    eye = (
        lax.broadcasted_iota(jnp.int32, (n, n), 0) == lax.broadcasted_iota(jnp.int32, (n, n), 1)
    ).astype(jnp.float32)
    w = jnp.concatenate([a, eye], axis=1)
    for k in range(0, n, 8):
        left = n - k
        cols = [jnp.broadcast_to(w[:, k + j:k + j + 1], (left, 2 * n)) for j in range(8)]
        for j in range(8):
            pivot = cols[j][j:j + 1, :]
            inv = lax.rsqrt(pivot)
            inv = inv * (1.5 - 0.5 * pivot * inv * inv)
            row = w[j:j + 1, :] * inv
            rows_ref[k + j:k + j + 1, :] = row
            below = cols[j] * inv
            w = w - below * row
            for m in range(j + 1, 8):
                cols[m] = cols[m] - below * (cols[m][j:j + 1, :] * inv)
        w = w[8:, :]
    return rows_ref[:, n:]


def row_order(rows, first, count):
    n = rows * count
    assert rows & (rows - 1) == 0
    at = lax.broadcasted_iota(jnp.int32, (n, n), 0)
    source = lax.shift_right_logical(at, rows.bit_length() - 1)
    r = at & (rows - 1)
    place = jnp.where(r < first, source * first + r, count * first + source * (rows - first) + r - first)
    return (place == lax.broadcasted_iota(jnp.int32, (n, n), 1)).astype(jnp.float32)


def orth(matrix, rows_ref):
    inverse = inverse_factor(contract(matrix, matrix, ((1,), (1,))), rows_ref)
    return contract(inverse, matrix, ((1,), (0,)))


def gram_kernel(
    nf, ng, first, sizes, scale, field, start, fib, out, held,
    part, r1, r2, r3, rows_ref, own_sem,
    a_send, a_recv, c_send, c_recv, z_send, z_recv,
):
    f = lax.axis_index("fibre")
    g = lax.axis_index("group")
    nz = nf // 2
    plane = 2 * ng
    core = lax.rem(f, 2)
    z = f // 2
    u = g * 2 + core
    rows, width = field.shape[0], fib.shape[1]

    def remote(src, dst, send, recv, slot, device):
        copy = pltpu.make_async_remote_copy(
            src_ref=src, dst_ref=dst, send_sem=send.at[slot], recv_sem=recv.at[slot],
            device_id=device, device_id_type=MESH,
        )
        copy.start()
        return copy

    def fibre_peer(o):
        return lax.rem(f + o, nf)

    def plane_peer(o):
        return lax.rem(u + o, plane)

    def plane_device(o):
        v = plane_peer(o)
        return (z * 2 + lax.rem(v, 2), v // 2)

    def z_device(o):
        return (lax.rem(z + o, nz) * 2 + core, g)

    barrier = pltpu.get_barrier_semaphore()
    for o in range(1, nf):
        pl.semaphore_signal(barrier, inc=1, device_id=(fibre_peer(o), g), device_id_type=MESH)
    for o in range(1, plane):
        pl.semaphore_signal(barrier, inc=1, device_id=plane_device(o), device_id_type=MESH)
    pl.semaphore_wait(barrier, nf + plane - 2)

    far_first = sorted(range(1, nf), key=lambda o: abs(o - nf // 2))
    bounds = ((0, first), (first, rows))
    sends, owns = [], []
    for c, (low, high) in enumerate(bounds):
        here = fib.at[aligned(nf * low + f * (high - low), high - low), :]
        sends.append([
            remote(
                field.at[low:high, pl.ds(pl.multiple_of(fibre_peer(o) * width, TILE), width)],
                here, a_send, a_recv, c * nf + o, (fibre_peer(o), g),
            )
            for o in far_first
        ])
        own = pltpu.make_async_copy(
            field.at[low:high, pl.ds(pl.multiple_of(f * width, TILE), width)], here, own_sem.at[c]
        )
        own.start()
        owns.append(own)

    held[...] = orth(contract(start[...], row_order(rows, first, nf), ((1,), (0,))), rows_ref)

    def summed(p):
        begin, size = sum(sizes[:p]), sizes[p]
        eighth = size // plane
        piece = eighth // nz
        at1 = 0 if p == 0 else r1.shape[1] - eighth
        at2 = 0 if p == 0 else r2.shape[1] - piece
        copies = [
            remote(part.at[aligned(begin + plane_peer(o) * eighth, eighth), :],
                   r1.at[o, at1:at1 + eighth, :], c_send, c_recv, 2 * p * plane + o, plane_device(o))
            for o in range(1, plane)
        ]
        yield
        for copy in copies:
            copy.wait()
        mine = begin + u * eighth
        total = part[aligned(mine, eighth), :]
        for o in range(1, plane):
            total += r1[o, at1:at1 + eighth, :]

        if p == 0:
            part[aligned(mine, eighth), :] = total
            copies = [
                remote(part.at[aligned(mine + lax.rem(z + o, nz) * piece, piece), :],
                       r2.at[o, at2:at2 + piece, :], z_send, z_recv, o, z_device(o))
                for o in range(1, nz)
            ]
            yield
            for copy in copies:
                copy.wait()
            last = mine + z * piece
            total = part[aligned(last, piece), :]
            for o in range(1, nz):
                total += r2[o, at2:at2 + piece, :]
            out[aligned(last, piece), :] = total * scale
            block = out.at[aligned(last, piece), :]
            copies = [
                remote(block, block, z_send, z_recv, nz + o, z_device(o)) for o in range(1, nz)
            ]
            yield
            for copy in copies:
                copy.wait()
        else:
            r3[z] = total
            copies = [
                remote(r3.at[z], r3.at[z], z_send, z_recv, 2 * nz + o, z_device(o))
                for o in range(1, nz)
            ]
            yield
            for copy in copies:
                copy.wait()
            total = r3[0]
            for n in range(1, nz):
                total += r3[n]
            out[aligned(mine, eighth), :] = total * scale

        block = out.at[aligned(mine, eighth), :]
        copies = [
            remote(block, block, c_send, c_recv, (2 * p + 1) * plane + o, plane_device(o))
            for o in range(1, plane)
        ]
        yield
        for copy in copies:
            copy.wait()

    going = []
    for c, (low, high) in enumerate(bounds):
        for copy in sends[c]:
            copy.wait_recv()
        owns[c].wait()
        begin = sum(sizes[:c])
        base = begin
        end = nf * high // TILE
        for pair in range(nf * low // TILE, end, 2):
            top = min(pair + 2, end)
            strip = contract(fib[pair * TILE:top * TILE, :], fib[:top * TILE, :], ((1,), (1,)))
            for i in range(pair, top):
                for j in range(i + 1):
                    part[base:base + TILE, :] = strip[(i - pair) * TILE:(i - pair + 1) * TILE, j * TILE:(j + 1) * TILE]
                    base += TILE
        if base < begin + sizes[c]:
            part[base:begin + sizes[c], :] = jnp.zeros((begin + sizes[c] - base, TILE), jnp.float32)
        step = summed(c)
        next(step)
        going.append(step)
        if c == 0:
            next(step)
    going.reverse()
    while going:
        for step in list(going):
            try:
                next(step)
            except StopIteration:
                going.remove(step)
    for copies in sends:
        for copy in copies:
            copy.wait_send()


def basis_kernel(nf, first, sizes, packed, fib, begin, basis, core, gram, held, rows_ref):
    order = fib.shape[0]
    split = nf * first // TILE
    base = 0
    for i in range(order // TILE):
        if i == split:
            base = sizes[0]
        for j in range(i + 1):
            block = packed[base:base + TILE, :]
            gram[i * TILE:(i + 1) * TILE, j * TILE:(j + 1) * TILE] = block
            if j < i:
                gram[j * TILE:(j + 1) * TILE, i * TILE:(i + 1) * TILE] = block.T
            base += TILE
    held[...] = begin[...]

    def iterate(step, carry):
        held[...] = orth(contract(held[...], gram[...], ((1,), (0,))), rows_ref)
        return carry

    lax.fori_loop(0, ITERS, iterate, 0)
    basis[...] = contract(held[...], row_order(order // nf, first, nf), ((1,), (1,)))
    core[...] = contract(held[...], fib[...], ((1,), (0,)))


def on_device(nf, ng, field, start):
    rows, columns = field.shape
    order, rank = start.shape
    width = columns // nf
    first = rows * 3 // 4 if rows % 32 == 0 else rows // 2
    blocks, early = order // TILE, nf * first // TILE
    unit = 8 * nf * ng
    counts = (early * (early + 1) // 2, blocks * (blocks + 1) // 2 - early * (early + 1) // 2)
    sizes = [-(-(n * TILE) // unit) * unit for n in counts]
    packed_rows = sum(sizes)
    plane, nz = 2 * ng, nf // 2
    vmem = pl.BlockSpec(memory_space=pltpu.VMEM)
    f32 = jnp.float32
    dma = pltpu.SemaphoreType.DMA
    fib, packed, begin = pl.pallas_call(
        functools.partial(gram_kernel, nf, ng, first, sizes, 1.0 / (columns * ng)),
        out_shape=(
            jax.ShapeDtypeStruct((order, width), f32),
            jax.ShapeDtypeStruct((packed_rows, TILE), f32),
            jax.ShapeDtypeStruct((rank, order), f32),
        ),
        in_specs=[pl.BlockSpec(memory_space=pl.ANY), vmem],
        out_specs=(vmem, vmem, vmem),
        scratch_shapes=[
            pltpu.VMEM((packed_rows, TILE), f32),
            pltpu.VMEM((plane, packed_rows // plane, TILE), f32),
            pltpu.VMEM((nz, sizes[0] // plane // nz, TILE), f32),
            pltpu.VMEM((nz, sizes[1] // plane, TILE), f32),
            pltpu.VMEM((rank, 2 * rank), f32),
            dma((2,)),
            dma((2 * nf,)), dma((2 * nf,)),
            dma((4 * plane,)), dma((4 * plane,)),
            dma((3 * nz,)), dma((3 * nz,)),
        ],
        compiler_params=pltpu.CompilerParams(
            collective_id=0, has_side_effects=True, vmem_limit_bytes=48 * 2**20
        ),
        name="gram",
    )(field, start.T)
    basis, core = pl.pallas_call(
        functools.partial(basis_kernel, nf, first, sizes),
        out_shape=(
            jax.ShapeDtypeStruct((rank, order), f32),
            jax.ShapeDtypeStruct((rank, width), f32),
        ),
        in_specs=[vmem] * 3,
        out_specs=(vmem, vmem),
        scratch_shapes=[
            pltpu.VMEM((order, order), f32),
            pltpu.VMEM((rank, order), f32),
            pltpu.VMEM((rank, 2 * rank), f32),
        ],
        compiler_params=pltpu.CompilerParams(vmem_limit_bytes=48 * 2**20),
        name="basis",
    )(packed, fib, begin)
    return basis.T, core


def solution(mesh):
    nf, ng = mesh.shape["fibre"], mesh.shape["group"]
    return jax.shard_map(
        functools.partial(on_device, nf, ng),
        mesh=mesh,
        in_specs=(P("fibre", "group"), P()),
        out_specs=(P(), P(None, ("group", "fibre"))),
        check_vma=False,
    )
```

time: 252 us -> 89.8 us (0.36)
  waiting for transfers between devices: 165 us -> 0 us
  Pallas kernels: 0 us -> 86.5 us
  other arithmetic: 48.3 us -> 0 us
  matrix products: 13.9 us -> 0 us
  between operations: 14.2 us -> 0.65 us
  starting transfers between devices: 6.36 us -> 0 us
    psum x1 -> x0, waiting for transfers between devices: 122 us -> none  [on_device(): gram_matrix = lax.psum(local_gram, ('fibre', 'group'))]
    pallas_call x0 -> x2, Pallas kernels: none -> 86.5 us  [the longest x1 74 us: on_device(): pl.pallas_call(functools.partial(gram_kernel, nf, ng, first, sizes, 1.0 /...]
    another operation x20 -> x0, other arithmetic: 48.3 us -> none  [the longest x12 26.1 us: orthonormal(): lower_factor = jnp.linalg.cholesky(inner_gram)]
    all_to_all x1 -> x0, waiting for transfers between devices: 42.8 us -> none  [on_device(): lax.all_to_all(species_field, 'fibre', split_axis=1, concat_axis=0, tiled...]
    dot_general x9 -> x0, matrix products: 12.6 us -> none  [the longest x3 4.9 us: on_device(): jnp.dot(gram_matrix, mode_basis, precision=highest_precision)]
    all_to_all x1 -> x0, starting transfers between devices: 6.33 us -> none  [on_device(): lax.all_to_all(species_field, 'fibre', split_axis=1, concat_axis=0, tiled...]
    all_to_all x1 -> x0, local copies, waits for them, and re-layouts: 3.23 us -> none  [on_device(): lax.all_to_all(species_field, 'fibre', split_axis=1, concat_axis=0, tiled...]
  transfers between devices with their start and end apart: 2 -> 0, of which waited for: 2 -> 0; matrix products, arithmetic and copies ran while one was open for 5% -> 0% of each run, Pallas kernels for 0% -> 0%
where the time goes in v3:
time: 89.8 us; the launch traced here: 89.7 us
  Pallas kernels  86.5 us (96%)
  local copies, waits for them, and re-layouts  2.49 us (3%)
    pallas_call x1, Pallas kernels, on_device(): pl.pallas_call(functools.partial(gram_kernel, nf, ng, first, sizes, 1.0 /...  74 us
    pallas_call x1, Pallas kernels, on_device(): pl.pallas_call(functools.partial(basis_kernel, nf, first, sizes), out_sha...  12.5 us
    unnamed x4, local copies, waits for them, and re-layouts  2.49 us

profile of v3, /device:TPU:0, one launch (start us, length us, event | category | flops | bytes accessed | tf_op | source)
XLA Modules:
  0.0 89.7 jit_solution(11461453014954233614)
XLA Ops:
  0.6 0.0 copy-start
  0.6 1.6 %copy-done = f32[64,8192]{1,0:T(8,128)S(1)} copy-done((f32[64,8192]{1,0:T(8,128)S(1)}, f32[64,8192]{1,0:T(8,128)}, u32[]{:S(2)}) %copy-start) | copy-done | bytes 2097176
  2.2 0.0 copy-start.1
  2.2 0.9 %copy-done.1 = f32[512,64]{0,1:T(8,128)S(1)} copy-done((f32[512,64]{0,1:T(8,128)S(1)}, f32[512,64]{0,1:T(8,128)}, u32[]{:S(2)}) %copy-start.1) | copy-done | bytes 131096
  3.1 74.0 %gram.1 = (f32[512,1024]{1,0:T(8,128)S(1)}, f32[1280,128]{1,0:T(8,128)S(1)}, f32[64,512]{1,0:T(8,128)S(1)}) custom-call(f32[64,8192]{1,0:T(8,128)S(1)} %copy-done, f32[64,512]{1,0:T(8,128)S(1)} %bitcast.2), custom_call_target="tpu_custom_call" | custom-call | tf_op jit(solution)/shard_map/gram/pallas_call | solution.py:262
  77.2 12.5 %basis.1 = (f32[64,512]{1,0:T(8,128)}, f32[64,1024]{1,0:T(8,128)}) custom-call(f32[1280,128]{1,0:T(8,128)S(1)} %get-tuple-element.7.packed, f32[512,1024]{1,0:T(8,128)S(1)} %get-tuple-element.8.fib, f32[64,512]{1,0:T(8,128)S(1)} %get-tuple-element.9.begin), custom_call_target="tpu_custom_call" | custom-call | tf_op jit(solution)/shard_map/basis/pallas_call | solution.py:287
Async XLA Ops:
  0.6 1.6 %copy-start = (f32[64,8192]{1,0:T(8,128)S(1)}, f32[64,8192]{1,0:T(8,128)}, u32[]{:S(2)}) copy-start(f32[64,8192]{1,0:T(8,128)} %field.1) | copy-start | bytes 6291460
  2.2 0.9 %copy-start.1 = (f32[512,64]{0,1:T(8,128)S(1)}, f32[512,64]{0,1:T(8,128)}, u32[]{:S(2)}) copy-start(f32[512,64]{0,1:T(8,128)} %param.3) | copy-start | bytes 393220

commit v4 on v3

--- a/solution.py
+++ b/solution.py
@@ -75,16 +75,21 @@
     u = g * 2 + core
     rows, width = field.shape[0], fib.shape[1]
 
-    def remote(src, dst, send, recv, slot, device):
+    def remote(src, dst, send, recv, slot, device, start=True):
         copy = pltpu.make_async_remote_copy(
             src_ref=src, dst_ref=dst, send_sem=send.at[slot], recv_sem=recv.at[slot],
             device_id=device, device_id_type=MESH,
         )
-        copy.start()
+        if start:
+            copy.start()
         return copy
 
     def fibre_peer(o):
-        return lax.rem(f + o, nf)
+        peer = f
+        for bit in range(o.bit_length()):
+            if o >> bit & 1:
+                peer = peer + 2**bit - 2 * 2**bit * lax.rem(f // 2**bit, 2)
+        return peer
 
     def plane_peer(o):
         return lax.rem(u + o, plane)
@@ -103,25 +108,43 @@
         pl.semaphore_signal(barrier, inc=1, device_id=plane_device(o), device_id_type=MESH)
     pl.semaphore_wait(barrier, nf + plane - 2)
 
-    far_first = sorted(range(1, nf), key=lambda o: abs(o - nf // 2))
+    assert nf & (nf - 1) == 0
+    inner = lax.rem((z + 1) // 2, 2)
+    near = [o for o in range(2, nf) if o < 4]
+    far = [o for o in range(2, nf) if o >= 4]
     bounds = ((0, first), (first, rows))
     sends, owns = [], []
     for c, (low, high) in enumerate(bounds):
         here = fib.at[aligned(nf * low + f * (high - low), high - low), :]
-        sends.append([
-            remote(
+        copies = {
+            o: remote(
                 field.at[low:high, pl.ds(pl.multiple_of(fibre_peer(o) * width, TILE), width)],
-                here, a_send, a_recv, c * nf + o, (fibre_peer(o), g),
+                here, a_send, a_recv, c * nf + o, (fibre_peer(o), g), start=False,
             )
-            for o in far_first
-        ])
+            for o in range(1, nf)
+        }
+
+        @pl.when(inner == 0)
+        def _():
+            for o in near + far + [1]:
+                copies[o].start()
+
+        @pl.when(inner == 1)
+        def _():
+            for o in far + near + [1]:
+                copies[o].start()
+
+        sends.append(list(copies.values()))
         own = pltpu.make_async_copy(
             field.at[low:high, pl.ds(pl.multiple_of(f * width, TILE), width)], here, own_sem.at[c]
         )
         own.start()
         owns.append(own)
 
-    held[...] = orth(contract(start[...], row_order(rows, first, nf), ((1,), (0,))), rows_ref)
+    begin = pltpu.make_async_copy(start, held, own_sem.at[2])
+    begin.start()
+    begin.wait()
+    held[...] = orth(contract(held[...], row_order(rows, first, nf), ((1,), (0,))), rows_ref)
 
     def summed(p):
         begin, size = sum(sizes[:p]), sizes[p]
@@ -207,8 +230,6 @@
         step = summed(c)
         next(step)
         going.append(step)
-        if c == 0:
-            next(step)
     going.reverse()
     while going:
         for step in list(going):
@@ -266,7 +287,7 @@
             jax.ShapeDtypeStruct((packed_rows, TILE), f32),
             jax.ShapeDtypeStruct((rank, order), f32),
         ),
-        in_specs=[pl.BlockSpec(memory_space=pl.ANY), vmem],
+        in_specs=[pl.BlockSpec(memory_space=pltpu.HBM)] * 2,
         out_specs=(vmem, vmem, vmem),
         scratch_shapes=[
             pltpu.VMEM((packed_rows, TILE), f32),
@@ -274,7 +295,7 @@
             pltpu.VMEM((nz, sizes[0] // plane // nz, TILE), f32),
             pltpu.VMEM((nz, sizes[1] // plane, TILE), f32),
             pltpu.VMEM((rank, 2 * rank), f32),
-            dma((2,)),
+            dma((3,)),
             dma((2 * nf,)), dma((2 * nf,)),
             dma((4 * plane,)), dma((4 * plane,)),
             dma((3 * nz,)), dma((3 * nz,)),

time: 89.8 us -> 90.2 us (level)
  no operation moved by 1% of the time
where the time goes in v4:
time: 90.2 us; the launch traced here: 90 us
  Pallas kernels  86.9 us (96%)
  local copies, waits for them, and re-layouts  2.49 us (3%)
    pallas_call x1, Pallas kernels, on_device(): pl.pallas_call(functools.partial(gram_kernel, nf, ng, first, sizes, 1.0 /...  74.4 us
    pallas_call x1, Pallas kernels, on_device(): pl.pallas_call(functools.partial(basis_kernel, nf, first, sizes), out_sha...  12.5 us
    unnamed x4, local copies, waits for them, and re-layouts  2.49 us

profile of v4, /device:TPU:0, one launch (start us, length us, event | category | flops | bytes accessed | tf_op | source)
XLA Modules:
  0.0 90.0 jit_solution(9051886266672633256)
XLA Ops:
  0.6 0.0 copy-start
  0.6 1.6 %copy-done = f32[64,8192]{1,0:T(8,128)S(1)} copy-done((f32[64,8192]{1,0:T(8,128)S(1)}, f32[64,8192]{1,0:T(8,128)}, u32[]{:S(2)}) %copy-start) | copy-done | bytes 2097176
  2.2 0.0 copy-start.1
  2.2 0.9 %copy-done.1 = f32[512,64]{0,1:T(8,128)S(1)} copy-done((f32[512,64]{0,1:T(8,128)S(1)}, f32[512,64]{0,1:T(8,128)}, u32[]{:S(2)}) %copy-start.1) | copy-done | bytes 131096
  3.1 74.4 %gram.1 = (f32[512,1024]{1,0:T(8,128)S(1)}, f32[1280,128]{1,0:T(8,128)S(1)}, f32[64,512]{1,0:T(8,128)S(1)}) custom-call(f32[64,8192]{1,0:T(8,128)S(1)} %copy-done, f32[64,512]{1,0:T(8,128)S(1)} %bitcast.2), custom_call_target="tpu_custom_call" | custom-call | tf_op jit(solution)/shard_map/gram/pallas_call | solution.py:283
  77.6 12.5 %basis.1 = (f32[64,512]{1,0:T(8,128)}, f32[64,1024]{1,0:T(8,128)}) custom-call(f32[1280,128]{1,0:T(8,128)S(1)} %get-tuple-element.7.packed, f32[512,1024]{1,0:T(8,128)S(1)} %get-tuple-element.8.fib, f32[64,512]{1,0:T(8,128)S(1)} %get-tuple-element.9.begin), custom_call_target="tpu_custom_call" | custom-call | tf_op jit(solution)/shard_map/basis/pallas_call | solution.py:308
Async XLA Ops:
  0.6 1.6 %copy-start = (f32[64,8192]{1,0:T(8,128)S(1)}, f32[64,8192]{1,0:T(8,128)}, u32[]{:S(2)}) copy-start(f32[64,8192]{1,0:T(8,128)} %field.1) | copy-start | bytes 6291460
  2.2 0.9 %copy-start.1 = (f32[512,64]{0,1:T(8,128)S(1)}, f32[512,64]{0,1:T(8,128)}, u32[]{:S(2)}) copy-start(f32[512,64]{0,1:T(8,128)} %param.3) | copy-start | bytes 393220

commit v5 on v4

--- a/solution.py
+++ b/solution.py
@@ -109,7 +109,6 @@
     pl.semaphore_wait(barrier, nf + plane - 2)
 
     assert nf & (nf - 1) == 0
-    inner = lax.rem((z + 1) // 2, 2)
     near = [o for o in range(2, nf) if o < 4]
     far = [o for o in range(2, nf) if o >= 4]
     bounds = ((0, first), (first, rows))
@@ -124,17 +123,10 @@
             for o in range(1, nf)
         }
 
-        @pl.when(inner == 0)
-        def _():
-            for o in near + far + [1]:
-                copies[o].start()
-
-        @pl.when(inner == 1)
-        def _():
+        if c == 0:
             for o in far + near + [1]:
                 copies[o].start()
-
-        sends.append(list(copies.values()))
+        sends.append(copies)
         own = pltpu.make_async_copy(
             field.at[low:high, pl.ds(pl.multiple_of(f * width, TILE), width)], here, own_sem.at[c]
         )
@@ -145,6 +137,10 @@
     begin.start()
     begin.wait()
     held[...] = orth(contract(held[...], row_order(rows, first, nf), ((1,), (0,))), rows_ref)
+
+    for o in [1] + near + far:
+        sends[0][o].wait_send()
+        sends[1][o].start()
 
     def summed(p):
         begin, size = sum(sizes[:p]), sizes[p]
@@ -212,7 +208,7 @@
 
     going = []
     for c, (low, high) in enumerate(bounds):
-        for copy in sends[c]:
+        for copy in sends[c].values():
             copy.wait_recv()
         owns[c].wait()
         begin = sum(sizes[:c])
@@ -230,6 +226,9 @@
         step = summed(c)
         next(step)
         going.append(step)
+        if c == 0:
+            next(step)
+            next(step)
     going.reverse()
     while going:
         for step in list(going):
@@ -237,9 +236,8 @@
                 next(step)
             except StopIteration:
                 going.remove(step)
-    for copies in sends:
-        for copy in copies:
-            copy.wait_send()
+    for copy in sends[1].values():
+        copy.wait_send()
 
 
 def basis_kernel(nf, first, sizes, packed, fib, begin, basis, core, gram, held, rows_ref):
@@ -301,7 +299,7 @@
             dma((3 * nz,)), dma((3 * nz,)),
         ],
         compiler_params=pltpu.CompilerParams(
-            collective_id=0, has_side_effects=True, vmem_limit_bytes=48 * 2**20
+            collective_id=0, has_side_effects=True, vmem_limit_bytes=50 * 2**20
         ),
         name="gram",
     )(field, start.T)

time: 90.2 us -> 89.8 us (level)
  local copies, waits for them, and re-layouts: 2.49 us -> 0.9 us
  Pallas kernels: 86.9 us -> 88.1 us
    unnamed x4 -> x2, local copies, waits for them, and re-layouts: 2.49 us -> 0.9 us
    pallas_call x1, Pallas kernels: 74.4 us -> 75.6 us  [on_device(): pl.pallas_call(functools.partial(gram_kernel, nf, ng, first, sizes, 1.0 /...]
where the time goes in v5:
time: 89.8 us; the launch traced here: 89.6 us
  Pallas kernels  88.1 us (98%)
  local copies, waits for them, and re-layouts  0.9 us (1%)
    pallas_call x1, Pallas kernels, on_device(): pl.pallas_call(functools.partial(gram_kernel, nf, ng, first, sizes, 1.0 /...  75.6 us
    pallas_call x1, Pallas kernels, on_device(): pl.pallas_call(functools.partial(basis_kernel, nf, first, sizes), out_sha...  12.5 us

profile of v5, /device:TPU:0, one launch (start us, length us, event | category | flops | bytes accessed | tf_op | source)
XLA Modules:
  0.0 89.6 jit_solution(17709004234609029707)
XLA Ops:
  0.6 0.0 copy-start
  0.6 0.9 copy-done
  1.5 75.6 %gram.1 = (f32[512,1024]{1,0:T(8,128)S(1)}, f32[1280,128]{1,0:T(8,128)S(1)}, f32[64,512]{1,0:T(8,128)S(1)}) custom-call(f32[64,8192]{1,0:T(8,128)} %field.1, f32[64,512]{1,0:T(8,128)S(1)} %bitcast.2), custom_call_target="tpu_custom_call" | custom-call | tf_op jit(solution)/shard_map/gram/pallas_call | solution.py:281
  77.1 12.5 %basis.1 = (f32[64,512]{1,0:T(8,128)}, f32[64,1024]{1,0:T(8,128)}) custom-call(f32[1280,128]{1,0:T(8,128)S(1)} %get-tuple-element.7.packed, f32[512,1024]{1,0:T(8,128)S(1)} %get-tuple-element.8.fib, f32[64,512]{1,0:T(8,128)S(1)} %get-tuple-element.9.begin), custom_call_target="tpu_custom_call" | custom-call | tf_op jit(solution)/shard_map/basis/pallas_call | solution.py:306
Async XLA Ops:
  0.6 0.9 %copy-start = (f32[512,64]{0,1:T(8,128)S(1)}, f32[512,64]{0,1:T(8,128)}, u32[]{:S(2)}) copy-start(f32[512,64]{0,1:T(8,128)} %param.3) | copy-start | bytes 393220

commit v6 on v2

--- a/solution.py
+++ b/solution.py
@@ -46,9 +46,23 @@
     return rows_ref[:, n:]
 
 
-def kernel(
-    nf, ng, chunks, parts, scale, field, start, basis, core_out,
-    fib, part, out, r1, r2, r3, gram, held, rows_ref, own_sem,
+def block_places(blocks):
+    places = {}
+    for pair in reversed(range(0, blocks, 2)):
+        for i in range(pair, min(pair + 2, blocks)):
+            for j in range(i + 1):
+                places[i, j] = len(places) * TILE
+    return places
+
+
+def orth(matrix, rows_ref):
+    inverse = inverse_factor(contract(matrix, matrix, ((1,), (1,))), rows_ref)
+    return contract(inverse, matrix, ((1,), (0,)))
+
+
+def gram_kernel(
+    nf, ng, chunks, parts, scale, field, start, fib, out, held,
+    part, r1, r2, r3, rows_ref, own_sem,
     a_send, a_recv, c_send, c_recv, g_send, g_recv, z_send, z_recv,
 ):
     f = lax.axis_index("fibre")
@@ -103,11 +117,7 @@
         own.start()
         owns.append(own)
 
-    def orth(matrix):
-        inverse = inverse_factor(contract(matrix, matrix, ((1,), (1,))), rows_ref)
-        return contract(inverse, matrix, ((1,), (0,)))
-
-    held[...] = orth(start[...])
+    held[...] = orth(start[...], rows_ref)
 
     def summed(p, first, size):
         half = size // 2
@@ -174,11 +184,7 @@
         copy.wait()
 
     blocks = order // TILE
-    places = {}
-    for pair in reversed(range(0, blocks, 2)):
-        for i in range(pair, min(pair + 2, blocks)):
-            for j in range(i + 1):
-                places[i, j] = len(places) * TILE
+    places = block_places(blocks)
     filled = len(places) * TILE
     if filled < part.shape[0]:
         part[filled:, :] = jnp.zeros((part.shape[0] - filled, TILE), jnp.float32)
@@ -212,22 +218,25 @@
             except StopIteration:
                 going.remove(step)
 
-    for (i, j), at in places.items():
-        block = out[at:at + TILE, :]
+    for copies in sends:
+        for copy in copies:
+            copy.wait_send()
+
+
+def basis_kernel(packed, fib, begin, basis, core, gram, rows_ref):
+    for (i, j), at in block_places(fib.shape[0] // TILE).items():
+        block = packed[at:at + TILE, :]
         gram[i * TILE:(i + 1) * TILE, j * TILE:(j + 1) * TILE] = block
         if j < i:
             gram[j * TILE:(j + 1) * TILE, i * TILE:(i + 1) * TILE] = block.T
+    basis[...] = begin[...]
 
     def iterate(step, carry):
-        held[...] = orth(contract(held[...], gram[...], ((1,), (0,))))
+        basis[...] = orth(contract(basis[...], gram[...], ((1,), (0,))), rows_ref)
         return carry
 
     lax.fori_loop(0, ITERS, iterate, 0)
-    basis[...] = held[...]
-    core_out[...] = contract(held[...], fib[...], ((1,), (0,)))
-    for copies in sends:
-        for copy in copies:
-            copy.wait_send()
+    core[...] = contract(basis[...], fib[...], ((1,), (0,)))
 
 
 def on_device(nf, ng, field, start):
@@ -244,23 +253,20 @@
     vmem = pl.BlockSpec(memory_space=pltpu.VMEM)
     f32 = jnp.float32
     dma = pltpu.SemaphoreType.DMA
-    basis, core = pl.pallas_call(
-        functools.partial(kernel, nf, ng, chunks, parts, 1.0 / (columns * ng)),
+    fib, packed, begin = pl.pallas_call(
+        functools.partial(gram_kernel, nf, ng, chunks, parts, 1.0 / (columns * ng)),
         out_shape=(
+            jax.ShapeDtypeStruct((order, width), f32),
+            jax.ShapeDtypeStruct((packed_rows, TILE), f32),
             jax.ShapeDtypeStruct((rank, order), f32),
-            jax.ShapeDtypeStruct((rank, width), f32),
         ),
-        in_specs=[pl.BlockSpec(memory_space=pl.ANY), vmem],
-        out_specs=(vmem, vmem),
+        in_specs=[pl.BlockSpec(memory_space=pltpu.HBM), vmem],
+        out_specs=(vmem, vmem, vmem),
         scratch_shapes=[
-            pltpu.VMEM((order, width), f32),
-            pltpu.VMEM((packed_rows, TILE), f32),
             pltpu.VMEM((packed_rows, TILE), f32),
             pltpu.VMEM((packed_rows // 2, TILE), f32),
             pltpu.VMEM((ng, packed_rows // 2 // ng, TILE), f32),
             pltpu.VMEM((nf // 2, packed_rows // nf // ng, TILE), f32),
-            pltpu.VMEM((order, order), f32),
-            pltpu.VMEM((rank, order), f32),
             pltpu.VMEM((rank, 2 * rank), f32),
             dma((chunks,)),
             dma((chunks * nf,)), dma((chunks * nf,)),
@@ -269,10 +275,22 @@
             dma((2 * nf,)), dma((2 * nf,)),
         ],
         compiler_params=pltpu.CompilerParams(
-            collective_id=0, has_side_effects=True, vmem_limit_bytes=56 * 2**20
+            collective_id=0, has_side_effects=True, vmem_limit_bytes=50 * 2**20
         ),
-        name="subspace",
+        name="gram",
     )(field, start.T)
+    basis, core = pl.pallas_call(
+        basis_kernel,
+        out_shape=(
+            jax.ShapeDtypeStruct((rank, order), f32),
+            jax.ShapeDtypeStruct((rank, width), f32),
+        ),
+        in_specs=[vmem] * 3,
+        out_specs=(vmem, vmem),
+        scratch_shapes=[pltpu.VMEM((order, order), f32), pltpu.VMEM((rank, 2 * rank), f32)],
+        compiler_params=pltpu.CompilerParams(vmem_limit_bytes=48 * 2**20),
+        name="basis",
+    )(packed, fib, begin)
     return basis.T, core
 
 

time: 88.5 us -> 85.2 us (0.963)
  local copies, waits for them, and re-layouts: 3.24 us -> 0.9 us
  Pallas kernels: 84.5 us -> 83.5 us
    unnamed x2, local copies, waits for them, and re-layouts: 3.24 us -> 0.9 us
    pallas_call x1 -> x2, Pallas kernels: 84.5 us -> 83.5 us  [the longest x1 72 us: on_device(): pl.pallas_call(functools.partial(gram_kernel, nf, ng, chunks, parts, 1.0...]
where the time goes in v6:
time: 85.2 us; the launch traced here: 85.1 us
  Pallas kernels  83.5 us (98%)
  local copies, waits for them, and re-layouts  0.9 us (1%)
    pallas_call x1, Pallas kernels, on_device(): pl.pallas_call(functools.partial(gram_kernel, nf, ng, chunks, parts, 1.0...  72 us
    pallas_call x1, Pallas kernels, on_device(): pl.pallas_call(basis_kernel, out_shape=(jax.ShapeDtypeStruct((rank, order...  11.5 us

profile of v6, /device:TPU:0, one launch (start us, length us, event | category | flops | bytes accessed | tf_op | source)
XLA Modules:
  0.0 85.1 jit_solution(8612819359277424149)
XLA Ops:
  0.6 0.0 copy-start
  0.6 0.9 %copy-done = f32[512,64]{0,1:T(8,128)S(1)} copy-done((f32[512,64]{0,1:T(8,128)S(1)}, f32[512,64]{0,1:T(8,128)}, u32[]{:S(2)}) %copy-start) | copy-done | bytes 131096
  1.5 72.0 %gram.1 = (f32[512,1024]{1,0:T(8,128)S(1)}, f32[1280,128]{1,0:T(8,128)S(1)}, f32[64,512]{1,0:T(8,128)S(1)}) custom-call(f32[64,8192]{1,0:T(8,128)} %field.1, f32[64,512]{1,0:T(8,128)S(1)} %bitcast.2), custom_call_target="tpu_custom_call" | custom-call | tf_op jit(solution)/shard_map/gram/pallas_call | solution.py:256
  73.6 11.5 %basis.1 = (f32[64,512]{1,0:T(8,128)}, f32[64,1024]{1,0:T(8,128)}) custom-call(f32[1280,128]{1,0:T(8,128)S(1)} %get-tuple-element.7.packed, f32[512,1024]{1,0:T(8,128)S(1)} %get-tuple-element.8.fib, f32[64,512]{1,0:T(8,128)S(1)} %get-tuple-element.9.begin), custom_call_target="tpu_custom_call" | custom-call | tf_op jit(solution)/shard_map/basis/pallas_call | solution.py:282
Async XLA Ops:
  0.6 0.9 %copy-start = (f32[512,64]{0,1:T(8,128)S(1)}, f32[512,64]{0,1:T(8,128)}, u32[]{:S(2)}) copy-start(f32[512,64]{0,1:T(8,128)} %param.3) | copy-start | bytes 393220

commit v7 on v6

--- a/solution.py
+++ b/solution.py
@@ -223,20 +223,28 @@
             copy.wait_send()
 
 
-def basis_kernel(packed, fib, begin, basis, core, gram, rows_ref):
+def basis_kernel(packed, fib, begin, basis, core, gram, held, rows_ref):
     for (i, j), at in block_places(fib.shape[0] // TILE).items():
         block = packed[at:at + TILE, :]
         gram[i * TILE:(i + 1) * TILE, j * TILE:(j + 1) * TILE] = block
         if j < i:
             gram[j * TILE:(j + 1) * TILE, i * TILE:(i + 1) * TILE] = block.T
-    basis[...] = begin[...]
+    held[...] = contract(begin[...], gram[...], ((1,), (0,)))
 
     def iterate(step, carry):
-        basis[...] = orth(contract(basis[...], gram[...], ((1,), (0,))), rows_ref)
+        matrix = held[...]
+        inner = contract(matrix, matrix, ((1,), (1,)))
+        after = contract(matrix, gram[...], ((1,), (0,)))
+        held[...] = contract(inverse_factor(inner, rows_ref), after, ((1,), (0,)))
         return carry
 
-    lax.fori_loop(0, ITERS, iterate, 0)
-    core[...] = contract(basis[...], fib[...], ((1,), (0,)))
+    lax.fori_loop(0, ITERS - 1, iterate, 0)
+    matrix = held[...]
+    inner = contract(matrix, matrix, ((1,), (1,)))
+    after = contract(matrix, fib[...], ((1,), (0,)))
+    inverse = inverse_factor(inner, rows_ref)
+    basis[...] = contract(inverse, matrix, ((1,), (0,)))
+    core[...] = contract(inverse, after, ((1,), (0,)))
 
 
 def on_device(nf, ng, field, start):
@@ -287,7 +295,11 @@
         ),
         in_specs=[vmem] * 3,
         out_specs=(vmem, vmem),
-        scratch_shapes=[pltpu.VMEM((order, order), f32), pltpu.VMEM((rank, 2 * rank), f32)],
+        scratch_shapes=[
+            pltpu.VMEM((order, order), f32),
+            pltpu.VMEM((rank, order), f32),
+            pltpu.VMEM((rank, 2 * rank), f32),
+        ],
         compiler_params=pltpu.CompilerParams(vmem_limit_bytes=48 * 2**20),
         name="basis",
     )(packed, fib, begin)

time: 85.2 us -> 83.1 us (0.975)
  Pallas kernels: 83.5 us -> 81.4 us
    pallas_call x1, Pallas kernels: 11.5 us -> 9.35 us  [on_device(): pl.pallas_call(basis_kernel, out_shape=(jax.ShapeDtypeStruct((rank, order...]
where the time goes in v7:
time: 83.1 us; the launch traced here: 82.9 us
  Pallas kernels  81.4 us (98%)
  local copies, waits for them, and re-layouts  0.9 us (1%)
    pallas_call x1, Pallas kernels, on_device(): pl.pallas_call(functools.partial(gram_kernel, nf, ng, chunks, parts, 1.0...  72 us
    pallas_call x1, Pallas kernels, on_device(): pl.pallas_call(basis_kernel, out_shape=(jax.ShapeDtypeStruct((rank, order...  9.35 us

profile of v7, /device:TPU:0, one launch (start us, length us, event | category | flops | bytes accessed | tf_op | source)
XLA Modules:
  0.0 82.9 jit_solution(5586600756795096868)
XLA Ops:
  0.6 0.0 copy-start
  0.6 0.9 %copy-done = f32[512,64]{0,1:T(8,128)S(1)} copy-done((f32[512,64]{0,1:T(8,128)S(1)}, f32[512,64]{0,1:T(8,128)}, u32[]{:S(2)}) %copy-start) | copy-done | bytes 131096
  1.5 72.0 %gram.1 = (f32[512,1024]{1,0:T(8,128)S(1)}, f32[1280,128]{1,0:T(8,128)S(1)}, f32[64,512]{1,0:T(8,128)S(1)}) custom-call(f32[64,8192]{1,0:T(8,128)} %field.1, f32[64,512]{1,0:T(8,128)S(1)} %bitcast.2), custom_call_target="tpu_custom_call" | custom-call | tf_op jit(solution)/shard_map/gram/pallas_call | solution.py:264
  73.6 9.3 %basis.1 = (f32[64,512]{1,0:T(8,128)}, f32[64,1024]{1,0:T(8,128)}) custom-call(f32[1280,128]{1,0:T(8,128)S(1)} %get-tuple-element.7.packed, f32[512,1024]{1,0:T(8,128)S(1)} %get-tuple-element.8.fib, f32[64,512]{1,0:T(8,128)S(1)} %get-tuple-element.9.begin), custom_call_target="tpu_custom_call" | custom-call | tf_op jit(solution)/shard_map/basis/pallas_call | solution.py:290
Async XLA Ops:
  0.6 0.9 %copy-start = (f32[512,64]{0,1:T(8,128)S(1)}, f32[512,64]{0,1:T(8,128)}, u32[]{:S(2)}) copy-start(f32[512,64]{0,1:T(8,128)} %param.3) | copy-start | bytes 393220

commit v8 on v7

--- a/solution.py
+++ b/solution.py
@@ -75,12 +75,13 @@
     order = fib.shape[0]
     span = width // chunks
 
-    def remote(src, dst, send, recv, slot, device):
+    def remote(src, dst, send, recv, slot, device, start=True):
         copy = pltpu.make_async_remote_copy(
             src_ref=src, dst_ref=dst, send_sem=send.at[slot], recv_sem=recv.at[slot],
             device_id=device, device_id_type=MESH,
         )
-        copy.start()
+        if start:
+            copy.start()
         return copy
 
     def fibre_peer(o):
@@ -100,6 +101,7 @@
     pl.semaphore_wait(barrier, nf + ng - 2)
 
     far_first = sorted(range(1, nf), key=lambda o: abs(o - nf // 2))
+    ahead = 2
     sends = []
     owns = []
     for c in range(chunks):
@@ -107,7 +109,7 @@
         sends.append([
             remote(
                 field.at[:, pl.ds(pl.multiple_of(fibre_peer(o) * width + c * span, TILE), span)],
-                here, a_send, a_recv, c * nf + o, (fibre_peer(o), g),
+                here, a_send, a_recv, c * nf + o, (fibre_peer(o), g), start=c < ahead,
             )
             for o in far_first
         ])
@@ -190,6 +192,10 @@
         part[filled:, :] = jnp.zeros((part.shape[0] - filled, TILE), jnp.float32)
     sums = []
     for c in range(chunks):
+        if c + ahead < chunks:
+            for now, later in reversed(list(zip(sends[c], sends[c + ahead]))):
+                now.wait_send()
+                later.start()
         for copy in sends[c]:
             copy.wait_recv()
         owns[c].wait()
@@ -218,7 +224,7 @@
             except StopIteration:
                 going.remove(step)
 
-    for copies in sends:
+    for copies in sends[-ahead:]:
         for copy in copies:
             copy.wait_send()
 

time: 83.1 us -> 84.5 us (1.017)
  Pallas kernels: 81.4 us -> 82.8 us
    pallas_call x1, Pallas kernels: 72 us -> 73.5 us  [on_device(): pl.pallas_call(functools.partial(gram_kernel, nf, ng, chunks, parts, 1.0...]
where the time goes in v8:
time: 84.5 us; the launch traced here: 84.3 us
  Pallas kernels  82.8 us (98%)
  local copies, waits for them, and re-layouts  0.9 us (1%)
    pallas_call x1, Pallas kernels, on_device(): pl.pallas_call(functools.partial(gram_kernel, nf, ng, chunks, parts, 1.0...  73.5 us
    pallas_call x1, Pallas kernels, on_device(): pl.pallas_call(basis_kernel, out_shape=(jax.ShapeDtypeStruct((rank, order...  9.35 us

profile of v8, /device:TPU:0, one launch (start us, length us, event | category | flops | bytes accessed | tf_op | source)
XLA Modules:
  0.0 84.3 jit_solution(18208251337186643910)
XLA Ops:
  0.6 0.0 copy-start
  0.6 0.9 %copy-done = f32[512,64]{0,1:T(8,128)S(1)} copy-done((f32[512,64]{0,1:T(8,128)S(1)}, f32[512,64]{0,1:T(8,128)}, u32[]{:S(2)}) %copy-start) | copy-done | bytes 131096
  1.5 73.5 %gram.1 = (f32[512,1024]{1,0:T(8,128)S(1)}, f32[1280,128]{1,0:T(8,128)S(1)}, f32[64,512]{1,0:T(8,128)S(1)}) custom-call(f32[64,8192]{1,0:T(8,128)} %field.1, f32[64,512]{1,0:T(8,128)S(1)} %bitcast.2), custom_call_target="tpu_custom_call" | custom-call | tf_op jit(solution)/shard_map/gram/pallas_call | solution.py:270
  75.0 9.3 %basis.1 = (f32[64,512]{1,0:T(8,128)}, f32[64,1024]{1,0:T(8,128)}) custom-call(f32[1280,128]{1,0:T(8,128)S(1)} %get-tuple-element.7.packed, f32[512,1024]{1,0:T(8,128)S(1)} %get-tuple-element.8.fib, f32[64,512]{1,0:T(8,128)S(1)} %get-tuple-element.9.begin), custom_call_target="tpu_custom_call" | custom-call | tf_op jit(solution)/shard_map/basis/pallas_call | solution.py:296
Async XLA Ops:
  0.6 0.9 %copy-start = (f32[512,64]{0,1:T(8,128)S(1)}, f32[512,64]{0,1:T(8,128)}, u32[]{:S(2)}) copy-start(f32[512,64]{0,1:T(8,128)} %param.3) | copy-start | bytes 393220

commit v9 on v7

--- a/solution.py
+++ b/solution.py
@@ -62,15 +62,16 @@
 
 def gram_kernel(
     nf, ng, chunks, parts, scale, field, start, fib, out, held,
-    part, r1, r2, r3, rows_ref, own_sem,
-    a_send, a_recv, c_send, c_recv, g_send, g_recv, z_send, z_recv,
+    part, r1, r2, rows_ref, own_sem,
+    a_send, a_recv, c_send, c_recv, z_send, z_recv,
 ):
     f = lax.axis_index("fibre")
     g = lax.axis_index("group")
     nz = nf // 2
     core = lax.rem(f, 2)
     z = f // 2
-    mate = f + 1 - 2 * core
+    plane = 2 * ng
+    u = g * 2 + core
     rows, width = field.shape[0], fib.shape[1]
     order = fib.shape[0]
     span = width // chunks
@@ -86,8 +87,12 @@
     def fibre_peer(o):
         return lax.rem(f + o, nf)
 
-    def group_device(o):
-        return (f, lax.rem(g + o, ng))
+    def plane_peer(o):
+        return lax.rem(u + o, plane)
+
+    def plane_device(o):
+        v = plane_peer(o)
+        return (z * 2 + lax.rem(v, 2), v // 2)
 
     def z_device(o):
         return (lax.rem(z + o, nz) * 2 + core, g)
@@ -95,9 +100,9 @@
     barrier = pltpu.get_barrier_semaphore()
     for o in range(1, nf):
         pl.semaphore_signal(barrier, inc=1, device_id=(fibre_peer(o), g), device_id_type=MESH)
-    for o in range(1, ng):
-        pl.semaphore_signal(barrier, inc=1, device_id=group_device(o), device_id_type=MESH)
-    pl.semaphore_wait(barrier, nf + ng - 2)
+    for o in range(1, plane):
+        pl.semaphore_signal(barrier, inc=1, device_id=plane_device(o), device_id_type=MESH)
+    pl.semaphore_wait(barrier, nf + plane - 2)
 
     far_first = sorted(range(1, nf), key=lambda o: abs(o - nf // 2))
     sends = []
@@ -120,37 +125,26 @@
     held[...] = orth(start[...], rows_ref)
 
     def summed(p, first, size):
-        half = size // 2
-        quarter = half // ng
-        piece = quarter // nz
-        mine = first + core * half
-        other = first + (1 - core) * half
-        copy = remote(part.at[aligned(other, half), :], r1.at[0:half, :] if p == 0 else r1.at[r1.shape[0] - half:, :],
-                      c_send, c_recv, 2 * p, (mate, g))
-        yield
-        copy.wait()
-        base1 = 0 if p == 0 else r1.shape[0] - half
-        part[aligned(mine, half), :] += r1[base1:base1 + half, :]
-
-        at2 = 0 if p == 0 else r2.shape[1] - quarter
+        eighth = size // plane
+        piece = eighth // nz
+        at1 = 0 if p == 0 else r1.shape[1] - eighth
+        at2 = 0 if p == 0 else r2.shape[1] - piece
         copies = [
-            remote(part.at[aligned(mine + lax.rem(g + o, ng) * quarter, quarter), :],
-                   r2.at[o, at2:at2 + quarter, :], g_send, g_recv, 2 * p * ng + o, group_device(o))
-            for o in range(1, ng)
+            remote(part.at[aligned(first + plane_peer(o) * eighth, eighth), :],
+                   r1.at[o, at1:at1 + eighth, :], c_send, c_recv, 2 * p * plane + o, plane_device(o))
+            for o in range(1, plane)
         ]
         yield
         for copy in copies:
             copy.wait()
-        mine = mine + g * quarter
-        total = part[aligned(mine, quarter), :]
-        for o in range(1, ng):
-            total += r2[o, at2:at2 + quarter, :]
-        part[aligned(mine, quarter), :] = total
-
-        at3 = 0 if p == 0 else r3.shape[1] - piece
+        mine = first + u * eighth
+        total = part[aligned(mine, eighth), :]
+        for o in range(1, plane):
+            total += r1[o, at1:at1 + eighth, :]
+        part[aligned(mine, eighth), :] = total
         copies = [
             remote(part.at[aligned(mine + lax.rem(z + o, nz) * piece, piece), :],
-                   r3.at[o, at3:at3 + piece, :], z_send, z_recv, 2 * p * nz + o, z_device(o))
+                   r2.at[o, at2:at2 + piece, :], z_send, z_recv, 2 * p * nz + o, z_device(o))
             for o in range(1, nz)
         ]
         yield
@@ -159,9 +153,8 @@
         last = mine + z * piece
         total = part[aligned(last, piece), :]
         for o in range(1, nz):
-            total += r3[o, at3:at3 + piece, :]
+            total += r2[o, at2:at2 + piece, :]
         out[aligned(last, piece), :] = total * scale
-
         block = out.at[aligned(last, piece), :]
         copies = [
             remote(block, block, z_send, z_recv, (2 * p + 1) * nz + o, z_device(o))
@@ -170,18 +163,14 @@
         yield
         for copy in copies:
             copy.wait()
-        block = out.at[aligned(mine, quarter), :]
+        block = out.at[aligned(mine, eighth), :]
         copies = [
-            remote(block, block, g_send, g_recv, (2 * p + 1) * ng + o, group_device(o))
-            for o in range(1, ng)
+            remote(block, block, c_send, c_recv, (2 * p + 1) * plane + o, plane_device(o))
+            for o in range(1, plane)
         ]
         yield
         for copy in copies:
             copy.wait()
-        block = out.at[aligned(first + core * half, half), :]
-        copy = remote(block, block, c_send, c_recv, 2 * p + 1, (mate, g))
-        yield
-        copy.wait()
 
     blocks = order // TILE
     places = block_places(blocks)
@@ -272,14 +261,12 @@
         out_specs=(vmem, vmem, vmem),
         scratch_shapes=[
             pltpu.VMEM((packed_rows, TILE), f32),
-            pltpu.VMEM((packed_rows // 2, TILE), f32),
-            pltpu.VMEM((ng, packed_rows // 2 // ng, TILE), f32),
+            pltpu.VMEM((2 * ng, packed_rows // 2 // ng, TILE), f32),
             pltpu.VMEM((nf // 2, packed_rows // nf // ng, TILE), f32),
             pltpu.VMEM((rank, 2 * rank), f32),
             dma((chunks,)),
             dma((chunks * nf,)), dma((chunks * nf,)),
-            dma((4,)), dma((4,)),
-            dma((4 * ng,)), dma((4 * ng,)),
+            dma((8 * ng,)), dma((8 * ng,)),
             dma((2 * nf,)), dma((2 * nf,)),
         ],
         compiler_params=pltpu.CompilerParams(

time: 83.1 us -> 85.4 us (1.028)
  Pallas kernels: 81.4 us -> 83.7 us
    pallas_call x1, Pallas kernels: 72 us -> 74.4 us  [on_device(): pl.pallas_call(functools.partial(gram_kernel, nf, ng, chunks, parts, 1.0...]
where the time goes in v9:
time: 85.4 us; the launch traced here: 85.3 us
  Pallas kernels  83.7 us (98%)
  local copies, waits for them, and re-layouts  0.9 us (1%)
    pallas_call x1, Pallas kernels, on_device(): pl.pallas_call(functools.partial(gram_kernel, nf, ng, chunks, parts, 1.0...  74.4 us
    pallas_call x1, Pallas kernels, on_device(): pl.pallas_call(basis_kernel, out_shape=(jax.ShapeDtypeStruct((rank, order...  9.35 us

profile of v9, /device:TPU:0, one launch (start us, length us, event | category | flops | bytes accessed | tf_op | source)
XLA Modules:
  0.0 85.3 jit_solution(13299060338732769973)
XLA Ops:
  0.6 0.0 copy-start
  0.6 0.9 %copy-done = f32[512,64]{0,1:T(8,128)S(1)} copy-done((f32[512,64]{0,1:T(8,128)S(1)}, f32[512,64]{0,1:T(8,128)}, u32[]{:S(2)}) %copy-start) | copy-done | bytes 131096
  1.5 74.4 %gram.1 = (f32[512,1024]{1,0:T(8,128)S(1)}, f32[1280,128]{1,0:T(8,128)S(1)}, f32[64,512]{1,0:T(8,128)S(1)}) custom-call(f32[64,8192]{1,0:T(8,128)} %field.1, f32[64,512]{1,0:T(8,128)S(1)} %bitcast.2), custom_call_target="tpu_custom_call" | custom-call | tf_op jit(solution)/shard_map/gram/pallas_call | solution.py:253
  75.9 9.3 %basis.1 = (f32[64,512]{1,0:T(8,128)}, f32[64,1024]{1,0:T(8,128)}) custom-call(f32[1280,128]{1,0:T(8,128)S(1)} %get-tuple-element.7.packed, f32[512,1024]{1,0:T(8,128)S(1)} %get-tuple-element.8.fib, f32[64,512]{1,0:T(8,128)S(1)} %get-tuple-element.9.begin), custom_call_target="tpu_custom_call" | custom-call | tf_op jit(solution)/shard_map/basis/pallas_call | solution.py:277
Async XLA Ops:
  0.6 0.9 %copy-start = (f32[512,64]{0,1:T(8,128)S(1)}, f32[512,64]{0,1:T(8,128)}, u32[]{:S(2)}) copy-start(f32[512,64]{0,1:T(8,128)} %param.3) | copy-start | bytes 393220

commit v10 on v7

--- a/solution.py
+++ b/solution.py
@@ -251,7 +251,7 @@
     rows, columns = field.shape
     order, rank = start.shape
     width = columns // nf
-    chunks = 4
+    chunks = 2
     blocks = order // TILE
     unit = 8 * nf * ng
     units = -(-(blocks * (blocks + 1) // 2 * TILE) // unit)

time: 83.1 us -> 83.2 us (level)
  no operation moved by 1% of the time
where the time goes in v10:
time: 83.2 us; the launch traced here: 83 us
  Pallas kernels  81.5 us (98%)
  local copies, waits for them, and re-layouts  0.9 us (1%)
    pallas_call x1, Pallas kernels, on_device(): pl.pallas_call(functools.partial(gram_kernel, nf, ng, chunks, parts, 1.0...  72.1 us
    pallas_call x1, Pallas kernels, on_device(): pl.pallas_call(basis_kernel, out_shape=(jax.ShapeDtypeStruct((rank, order...  9.34 us

profile of v10, /device:TPU:0, one launch (start us, length us, event | category | flops | bytes accessed | tf_op | source)
XLA Modules:
  0.0 83.0 jit_solution(8242127298266186470)
XLA Ops:
  0.6 0.0 copy-start
  0.6 0.9 %copy-done = f32[512,64]{0,1:T(8,128)S(1)} copy-done((f32[512,64]{0,1:T(8,128)S(1)}, f32[512,64]{0,1:T(8,128)}, u32[]{:S(2)}) %copy-start) | copy-done | bytes 131096
  1.5 72.1 %gram.1 = (f32[512,1024]{1,0:T(8,128)S(1)}, f32[1280,128]{1,0:T(8,128)S(1)}, f32[64,512]{1,0:T(8,128)S(1)}) custom-call(f32[64,8192]{1,0:T(8,128)} %field.1, f32[64,512]{1,0:T(8,128)S(1)} %bitcast.2), custom_call_target="tpu_custom_call" | custom-call | tf_op jit(solution)/shard_map/gram/pallas_call | solution.py:264
  73.7 9.3 %basis.1 = (f32[64,512]{1,0:T(8,128)}, f32[64,1024]{1,0:T(8,128)}) custom-call(f32[1280,128]{1,0:T(8,128)S(1)} %get-tuple-element.7.packed, f32[512,1024]{1,0:T(8,128)S(1)} %get-tuple-element.8.fib, f32[64,512]{1,0:T(8,128)S(1)} %get-tuple-element.9.begin), custom_call_target="tpu_custom_call" | custom-call | tf_op jit(solution)/shard_map/basis/pallas_call | solution.py:290
Async XLA Ops:
  0.6 0.9 %copy-start = (f32[512,64]{0,1:T(8,128)S(1)}, f32[512,64]{0,1:T(8,128)}, u32[]{:S(2)}) copy-start(f32[512,64]{0,1:T(8,128)} %param.3) | copy-start | bytes 393220
